TPU v7x, 32 devices: a whole 2x2x4 slice. The times are simulated.
32 devices in a mesh: lat: 8 (over z, x), deg: 4 (over y, core).
Axes of the slice: x: 2, y: 2, z: 4, core: 2. Of those that a mesh axis runs over, the one named last changes fastest.
Arguments:
- eta_tl: float32 [64, 10752], P('lat'), may hold values from -6 to 6
- vel_tl: float32 [2, 64, 10752], P(None, 'lat'), may hold values from -6 to 6
- eta_adj: float32 [64, 10752], P('lat'), may hold values from -6 to 6
- vel_adj: float32 [2, 64, 10752], P(None, 'lat'), may hold values from -6 to 6
- depth: float32 [64, 10752], P('lat'), may hold values from 0.2 to 1
- drag: float32 [64, 10752], P('lat'), may hold values from 0.01 to 0.3
- ocean: int32 [64, 10752], P('lat'), may hold values 0 or 1
- basis: bfloat16 [1024, 64, 1024], P('lat', None, 'deg'), may hold values from -5 to 5
- love: float32 [1024], P('deg'), may hold values from 0.05 to 0.5
Outputs:
- eta_tl_out: float32 [64, 10752], P('lat')
- vel_tl_out: float32 [2, 64, 10752], P(None, 'lat')
- eta_adj_out: float32 [64, 10752], P('lat')
- vel_adj_out: float32 [2, 64, 10752], P(None, 'lat')
All inputs are finite; a program needn't handle non-finite values. No bound on the sum of `ocean` on one device may be relied on, other than what follows from the above.
Results may differ from a plain program's by a relative error of at most 0.02.
Values may be sent and summed in bfloat16 or wider, within the bound.
A program may use at most 320 MiB of HBM per device.

v0:
```python
import jax
import jax.numpy as jnp
import numpy as np
from jax import lax
from jax.sharding import PartitionSpec as P

STEPS = 2
LANES = 128
kappa_x = 0.3
kappa_y = 0.4


def passed_along(value, axis, by):
    length = lax.axis_size(axis)
    pairs = [(i, i + by) for i in range(length) if 0 <= i + by < length]
    return lax.ppermute(value, axis, pairs)


def circle(numerator, period):
    angles = 2.0 * np.pi * (numerator % period) / period
    return (np.cos(angles), np.sin(angles))


def fourier_tables(lon_count, order_total):
    major = lon_count // LANES
    blocks = -(-order_total // major)
    residues, lanes = (np.arange(major), np.arange(LANES))
    outer = np.stack(circle(residues[:, None] * residues[None, :], major))
    turn = np.stack(circle(residues[:, None] * lanes[None, :], lon_count))
    inner = np.stack(circle(np.arange(blocks)[:, None] * lanes[None, :], LANES))
    return (
        jnp.asarray(outer, jnp.bfloat16),
        jnp.asarray(turn, jnp.float32),
        jnp.asarray(inner, jnp.bfloat16),
    )


def order_factor(orders):
    return jnp.where(orders == 0, 1.0, 2.0).astype(jnp.bfloat16)


def analyse(stacked, analysis_weight, tables, order_count):
    outer, turn, inner = tables
    row_count = stacked.shape[1]
    lon_count = stacked.shape[2]
    split_rows = stacked.astype(jnp.bfloat16).reshape(2 * row_count, lon_count // LANES, LANES)
    first = jnp.einsum("cka,rab->crkb", outer, split_rows, preferred_element_type=jnp.float32)
    turned = jnp.stack(
        [first[0] * turn[0] - first[1] * turn[1], first[1] * turn[0] + first[0] * turn[1]]
    ).astype(jnp.bfloat16)
    second = jnp.stack([jnp.stack([inner[0], -inner[1]]), jnp.stack([inner[1], inner[0]])])
    spectra = jnp.einsum("crkb,dcnb->dnkr", turned, second, preferred_element_type=jnp.float32)
    spectra = spectra.reshape(2, -1, 2, row_count)[:, :order_count] * (1.0 / lon_count)
    return (spectra * analysis_weight[None, None, :, :]).astype(jnp.bfloat16)


def legendre(spectra, basis, love):
    coeffs = jnp.einsum("cmfi,mil->cmfl", spectra, basis, preferred_element_type=jnp.float32)
    scaled = (coeffs * love[None, None, None, :]).astype(jnp.bfloat16)
    return jnp.einsum("cmfl,mil->cmfi", scaled, basis, preferred_element_type=jnp.float32)


def synthesise(coeffs, factors, tables, output_weight):
    outer, turn, inner = tables
    major, blocks = (turn.shape[1], inner.shape[1])
    order_count = coeffs.shape[1]
    row_count = coeffs.shape[3]
    scaled = coeffs * factors[None, :, None, None]
    padded = jnp.pad(scaled, ((0, 0), (0, major * blocks - order_count), (0, 0), (0, 0)))
    padded = padded.reshape(2, blocks, major, 2 * row_count)
    second = jnp.stack([jnp.stack([inner[0], inner[1]]), jnp.stack([-inner[1], inner[0]])])
    first = jnp.einsum("cnkr,dcnb->drkb", padded, second, preferred_element_type=jnp.float32)
    turned = jnp.stack(
        [first[0] * turn[0] + first[1] * turn[1], first[1] * turn[0] - first[0] * turn[1]]
    ).astype(jnp.bfloat16)
    grid_out = jnp.einsum("cka,crkb->rab", outer, turned, preferred_element_type=jnp.float32)
    return grid_out.reshape(2, row_count, -1) * output_weight[:, :, None]


def edges_from(rows, by):
    sent = jnp.concatenate(rows, 0).astype(jnp.bfloat16)
    got = passed_along(sent, "lat", by).astype(jnp.float32)
    return [got[i : i + 1] for i in range(len(rows))]


def northward(values, edge):
    return jnp.concatenate([values[1:], edge], 0)


def southward(values, edge):
    return jnp.concatenate([edge, values[:-1]], 0)


def on_device(eta_tl, vel_tl, eta_adj, vel_adj, depth, drag, ocean, basis, love):
    row_count = eta_tl.shape[0]
    lon_count = eta_tl.shape[1]
    lat_count = lax.axis_size("lat")
    total_rows = row_count * lat_count
    first_row = lax.axis_index("lat") * row_count
    indices = first_row + jnp.arange(row_count, dtype=jnp.int32)
    latitude = (indices.astype(jnp.float32) + 0.5) * (jnp.pi / total_rows) - 0.5 * jnp.pi
    cosine = jnp.cos(latitude)
    quad_weight = jnp.pi / total_rows * cosine
    east_factor = (kappa_x / (0.5 + 0.5 * cosine))[:, None]
    wet_mask = ocean.astype(jnp.float32)
    flux_north = kappa_y * wet_mask * eta_adj
    north_depth, north_wet, north_flux = edges_from([depth[:1], wet_mask[:1], flux_north[:1]], -1)
    depth_up = northward(depth, north_depth)
    wet_up = northward(wet_mask, north_wet)
    mask_u = wet_mask * jnp.roll(wet_mask, -1, 1)
    mask_v = wet_mask * wet_up
    depth_u = 0.5 * (depth + jnp.roll(depth, -1, 1))
    depth_v = 0.5 * (depth + depth_up)
    retain = 1.0 - drag
    ones_weight = jnp.ones_like(quad_weight)
    analysis_weight = jnp.stack([quad_weight, ones_weight])
    output_weight = jnp.stack([ones_weight, quad_weight])
    owned_count = basis.shape[0]
    order_total = owned_count * lat_count
    full_orders = jnp.arange(order_total, dtype=jnp.int32)
    tables = fourier_tables(lon_count, order_total)
    full_factor = order_factor(full_orders)
    state_eta, state_vel = (eta_tl, vel_tl)
    back_eta, back_vel = (eta_adj, vel_adj)

    def adjoint_terms(eta, vel, flux_edge):
        flux_east = east_factor * wet_mask * eta
        flux_up = kappa_y * wet_mask * eta
        north_up = northward(flux_up, flux_edge)
        p_term = mask_u * (vel[0] + depth_u * (jnp.roll(flux_east, -1, 1) - flux_east))
        q_term = mask_v * (vel[1] + depth_v * (north_up - flux_up))
        return (p_term, q_term)

    p_term, q_term = adjoint_terms(back_eta, back_vel, north_flux)
    (q_edge,) = edges_from([q_term[-1:]], 1)
    for step_index in range(STEPS):
        flux_p = east_factor * p_term
        q_down = southward(q_term, q_edge)
        psi_bar = flux_p - jnp.roll(flux_p, 1, 1) + kappa_y * (q_term - q_down)
        spectra = analyse(jnp.stack([state_eta, psi_bar]), analysis_weight, tables, order_total)
        owned_rows = lax.all_to_all(spectra, "lat", split_axis=1, concat_axis=3, tiled=True)
        partial_value = legendre(owned_rows, basis, love)
        total_sum = lax.psum(partial_value.astype(jnp.bfloat16), "deg")
        banded = lax.all_to_all(total_sum, "lat", split_axis=3, concat_axis=1, tiled=True)
        loads = synthesise(banded, full_factor, tables, output_weight)
        last = step_index == STEPS - 1
        psi_now = state_eta - loads[0]
        back_eta = back_eta + psi_bar - loads[1]
        back_vel = (retain * p_term, retain * q_term)
        north_rows = [psi_now[:1]]
        if not last:
            north_rows.append(kappa_y * wet_mask[:1] * back_eta[:1])
        north_edges = edges_from(north_rows, -1)
        psi_up = northward(psi_now, north_edges[0])
        new_u = mask_u * (
            retain * state_vel[0] - east_factor * (jnp.roll(psi_now, -1, 1) - psi_now)
        )
        new_v = mask_v * (retain * state_vel[1] - kappa_y * (psi_up - psi_now))
        flux_x = depth_u * new_u
        flux_y = depth_v * new_v
        south_rows = [flux_y[-1:]]
        if not last:
            p_term, q_term = adjoint_terms(back_eta, back_vel, north_edges[1])
            south_rows.append(q_term[-1:])
        south_edges = edges_from(south_rows, 1)
        flux_down = southward(flux_y, south_edges[0])
        if not last:
            q_edge = south_edges[1]
        state_eta = state_eta - wet_mask * (
            east_factor * (flux_x - jnp.roll(flux_x, 1, 1)) + kappa_y * (flux_y - flux_down)
        )
        state_vel = (new_u, new_v)
    state_vel, back_vel = (jnp.stack(state_vel), jnp.stack(back_vel))
    return (state_eta, state_vel, back_eta, back_vel)


def solution(mesh):
    in_specs = (
        P("lat", None),
        P(None, "lat", None),
        P("lat", None),
        P(None, "lat", None),
        P("lat", None),
        P("lat", None),
        P("lat", None),
        P("lat", None, "deg"),
        P("deg"),
    )
    out_specs = (P("lat", None), P(None, "lat", None), P("lat", None), P(None, "lat", None))
    return jax.shard_map(
        on_device, mesh=mesh, in_specs=in_specs, out_specs=out_specs, check_vma=False
    )
```

profile of v0, /device:TPU:0, one launch (start us, length us, event | category | flops | bytes accessed | tf_op | source)
XLA Modules:
  0.0 200.0 jit_solution(16623130963314955521)
XLA Ops:
  7.3 1.0 slice.442
  8.3 1.0 convert_element_type.99
  9.3 1.3 multiply_multiply_fusion.3
  10.8 1.3 collective-permute-start
  12.8 0.5 copy-done.4
  13.4 4.8 %collective-permute-done = bf16[3,10752]{1,0:T(4,128)(2,1)S(1)} collective-permute-done((bf16[3,10752]{1,0:T(4,128)(2,1)S(1)}, bf16[3,10752]{1,0:T(4,128)(2,1)S(1)}, u32[]{:S(2)}, u32[]{:S(2)}) %collective-permute-start) | collective-permute-done | bytes 64544 | tf_op jit(solution)/shard_map/ppermute | solution.py:16
  18.3 1.3 broadcast_multiply_fusion.3
  19.7 4.8 %collective-permute-start.1 = (bf16[1,10752]{1,0:T(2,128)(2,1)S(1)}, bf16[1,10752]{1,0:T(2,128)(2,1)S(1)}, u32[]{:S(2)}, u32[]{:S(2)}) collective-permute-start(bf16[1,10752]{1,0:T(2,128)(2,1)S(1)} %slice.440), channel_id=1, source_target_pairs={{0,4},{4,8},{8,12},{12,16},{16,20},{20,24},{24,28},{1,5},{5,9},{9,... | collective-permute-start | bytes 64520 | tf_op jit(solution)/shard_map/ppermute | solution.py:16
  24.6 1.6 collective-permute-done.1
  26.2 0.9 convert_bitcast_fusion.2
  28.1 0.5 copy-done.33
  29.3 0.7 copy.57
  30.0 1.1 reshape.104
  31.1 12.4 %all_to_all.72 = bf16[8,2,2048]{2,1,0:T(2,128)(2,1)S(1)} all-to-all(bf16[8,2,2048]{2,1,0:T(2,128)(2,1)S(1)} %reshape.104), channel_id=1, replica_groups=mesh['lat'=8,'deg'=4] {'lat'}, dimensions={0} | all-to-all | bytes 131072 | tf_op jit(solution)/shard_map/all_to_all | solution.py:141
  43.5 1.2 reshape.105
  44.7 1.3 copy.90
  46.2 6.0 %fusion.45 = bf16[2,128,2,64]{3,2,0,1:T(2,128)(2,1)} fusion(bf16[128,64,256]{2,1,0:T(8,128)(2,1)} %param.19, bf16[2,128,2,64]{3,2,0,1:T(2,128)(2,1)S(1)} %copy.60, f32[256]{0:T(256)S(1)} %copy-done.31), kind=kOutput, calls=%fused_computation.25 | convolution fusion | flops 33849344 | bytes 4326400 | tf_op jit(solution)/shard_map/cmfl,mil->cmfi/dot_general | solution.py:60
  52.2 29.1 %all-reduce.7.cloned.1.call-done = bf16[2,128,2,64]{3,2,0,1:T(2,128)(2,1)} async-done(((bf16[2,128,2,64]{3,2,0,1:T(2,128)(2,1)}), bf16[2,128,2,64]{3,2,0,1:T(2,128)(2,1)}) %all-reduce.7.cloned.1.call-update) | async-done | bytes 65552 | tf_op jit(solution)/shard_map/psum | solution.py:143
  81.3 1.7 copy.61
  83.0 5.5 %all-to-all-start.1 = ((bf16[2,128,2,64]{1,2,0,3:T(2,128)(2,1)}), bf16[2,128,2,64]{1,2,0,3:T(2,128)(2,1)S(1)}, u32[]{:S(2)}, u32[]{:S(2)}) async-start(bf16[2,128,2,64]{1,2,0,3:T(2,128)(2,1)} %copy.61), calls=%async_computation.1 | async-start | bytes 131072 | tf_op jit(solution)/shard_map/all_to_all | solution.py:144
  88.5 6.8 %all-to-all-done.1 = bf16[2,128,2,64]{1,2,0,3:T(2,128)(2,1)S(1)} async-done(((bf16[2,128,2,64]{1,2,0,3:T(2,128)(2,1)}), bf16[2,128,2,64]{1,2,0,3:T(2,128)(2,1)S(1)}, u32[]{:S(2)}, u32[]{:S(2)}) %all-to-all-start.1) | async-done | bytes 65568 | tf_op jit(solution)/shard_map/all_to_all | solution.py:144
  96.8 0.8 copy-done.12
  98.0 0.7 copy-done.2
  98.9 1.3 collective-permute-start.2
  100.2 0.9 multiply_bitcast_fusion.1
  101.4 3.5 %collective-permute-done.2 = bf16[2,10752]{1,0:T(2,128)(2,1)S(1)} collective-permute-done((bf16[2,10752]{1,0:T(2,128)(2,1)S(1)}, bf16[2,10752]{1,0:T(2,128)(2,1)S(1)}, u32[]{:S(2)}, u32[]{:S(2)}) %collective-permute-start.2) | collective-permute-done | bytes 43040 | tf_op jit(solution)/shard_map/ppermute | solution.py:16
  104.9 1.3 fusion.128
  106.5 3.4 %collective-permute-start.3 = (bf16[2,10752]{1,0:T(2,128)(2,1)S(1)}, bf16[2,10752]{1,0:T(2,128)(2,1)S(1)}, u32[]{:S(2)}, u32[]{:S(2)}) collective-permute-start(bf16[2,10752]{1,0:T(2,128)(2,1)S(1)} %pad_maximum_fusion.6), channel_id=1, source_target_pairs={{0,4},{4,8},{8,12},{12,16},{16,20},{20,24},{24,28},{1,5},{5,9},{9,... | collective-permute-start | bytes 129032 | tf_op jit(solution)/shard_map/ppermute | solution.py:16
  110.0 1.3 collective-permute-done.3
  114.0 0.7 copy.66
  114.7 1.1 reshape.106
  115.8 10.6 %all_to_all.73 = bf16[8,2,2048]{2,1,0:T(2,128)(2,1)S(1)} all-to-all(bf16[8,2,2048]{2,1,0:T(2,128)(2,1)S(1)} %reshape.106), channel_id=1, replica_groups=mesh['lat'=8,'deg'=4] {'lat'}, dimensions={0} | all-to-all | bytes 131072 | tf_op jit(solution)/shard_map/all_to_all | solution.py:141
  126.4 1.2 reshape.107
  127.6 1.3 copy.96
  129.1 6.0 %fusion.40 = bf16[2,128,2,64]{3,2,0,1:T(2,128)(2,1)} fusion(bf16[128,64,256]{2,1,0:T(8,128)(2,1)} %param.19, bf16[2,128,2,64]{3,2,0,1:T(2,128)(2,1)S(1)} %copy.69, f32[256]{0:T(256)S(1)} %copy-done.32), kind=kOutput, calls=%fused_computation.24 | convolution fusion | flops 33849344 | bytes 4326400 | tf_op jit(solution)/shard_map/cmfl,mil->cmfi/dot_general | solution.py:60
  135.1 28.1 %all-reduce.9.cloned.1.call-done = bf16[2,128,2,64]{3,2,0,1:T(2,128)(2,1)} async-done(((bf16[2,128,2,64]{3,2,0,1:T(2,128)(2,1)}), bf16[2,128,2,64]{3,2,0,1:T(2,128)(2,1)}) %all-reduce.9.cloned.1.call-update) | async-done | bytes 65552 | tf_op jit(solution)/shard_map/psum | solution.py:143
  163.2 1.0 copy.70
  164.3 12.2 %all_to_all.74 = bf16[2,128,2,64]{1,2,0,3:T(2,128)(2,1)S(1)} all-to-all(bf16[2,128,2,64]{1,2,0,3:T(2,128)(2,1)S(1)} %copy.70), channel_id=1, replica_groups=mesh['lat'=8,'deg'=4] {'lat'}, dimensions={3} | all-to-all | bytes 131072 | tf_op jit(solution)/shard_map/all_to_all | solution.py:144
  177.7 1.0 reshape.83
  178.6 1.2 broadcast_multiply_fusion
  179.9 0.8 fusion.62
  180.8 1.4 collective-permute-start.4
  182.2 0.9 pad_maximum_fusion.1
  183.3 3.5 %collective-permute-done.4 = bf16[1,10752]{1,0:T(2,128)(2,1)S(1)} collective-permute-done((bf16[1,10752]{1,0:T(2,128)(2,1)S(1)}, bf16[1,10752]{1,0:T(2,128)(2,1)S(1)}, u32[]{:S(2)}, u32[]{:S(2)}) %collective-permute-start.4) | collective-permute-done | bytes 21536 | tf_op jit(solution)/shard_map/ppermute | solution.py:16
  187.3 3.2 %collective-permute-start.5 = (bf16[1,10752]{1,0:T(2,128)(2,1)S(1)}, bf16[1,10752]{1,0:T(2,128)(2,1)S(1)}, u32[]{:S(2)}, u32[]{:S(2)}) collective-permute-start(bf16[1,10752]{1,0:T(2,128)(2,1)S(1)} %slice.435), channel_id=1, source_target_pairs={{0,4},{4,8},{8,12},{12,16},{16,20},{20,24},{24,28},{1,5},{5,9},{9,... | collective-permute-start | bytes 64520 | tf_op jit(solution)/shard_map/ppermute | solution.py:16
  190.5 0.9 pad_maximum_fusion
  191.4 0.7 collective-permute-done.5
  192.2 0.9 fusion.101
  (151 shorter events, 10.2 us)
Async XLA Ops:
  7.2 74.1 %all-reduce.7.cloned.1.call-start = ((), (), s32[]{:S(2)}) async-start(), calls=%async_computation.4 | async-start | bytes 262144 | tf_op jit(solution)/shard_map/psum | solution.py:143
  9.3 3.1 %copy-start.1 = (f32[8,10752]{1,0:T(8,128)}, f32[8,10752]{1,0:T(8,128)S(1)}, u32[]{:S(2)}) copy-start(f32[8,10752]{1,0:T(8,128)S(1)} %convert_element_type.99) | copy-start | bytes 1032196
  9.3 3.0 %copy-start.3 = (f32[8,10752]{1,0:T(8,128)S(1)}, f32[8,10752]{1,0:T(8,128)}, u32[]{:S(2)}) copy-start(f32[8,10752]{1,0:T(8,128)} %param.16) | copy-start | bytes 1032196
  10.8 7.4 %collective-permute-start = (bf16[3,10752]{1,0:T(4,128)(2,1)S(1)}, bf16[3,10752]{1,0:T(4,128)(2,1)S(1)}, u32[]{:S(2)}, u32[]{:S(2)}) collective-permute-start(bf16[3,10752]{1,0:T(4,128)(2,1)S(1)} %pad_maximum_fusion.4), channel_id=1, source_target_pairs={{4,0},{8,4},{12,8},{16,12},{20,16},{24,20},{28,24},{5,1},{9,5},{13... | collective-permute-start | bytes 193544 | tf_op jit(solution)/shard_map/ppermute | solution.py:16
  12.4 1.0 copy-start.4
  12.5 5.8 %copy-start = (s32[8,10752]{1,0:T(8,128)S(1)}, s32[8,10752]{1,0:T(8,128)}, u32[]{:S(2)}) copy-start(s32[8,10752]{1,0:T(8,128)} %param.18) | copy-start | bytes 1032196
  12.5 5.8 %slice-start = ((f32[8,10752]{1,0:T(8,128)}), f32[8,1]{1,0:T(8,128)S(1)}, s32[]{:S(2)}) async-start(f32[8,10752]{1,0:T(8,128)} %copy-done.1), calls=%async_computation.6 | async-start | bytes 8192 | tf_op jit(solution)/shard_map/jit(_roll_static)/slice | solution.py:110
  12.5 5.8 %slice-start.1 = ((f32[8,10752]{1,0:T(8,128)}), f32[8,1]{1,0:T(8,128)S(1)}, s32[]{:S(2)}) async-start(f32[8,10752]{1,0:T(8,128)} %param.16), calls=%async_computation.7 | async-start | bytes 8192 | tf_op jit(solution)/shard_map/jit(_roll_static)/slice | solution.py:112
  12.6 5.8 %copy-start.23 = (f32[2,8,10752]{2,1,0:T(8,128)S(1)}, f32[2,8,10752]{2,1,0:T(8,128)}, u32[]{:S(2)}) copy-start(f32[2,8,10752]{2,1,0:T(8,128)} %param.15) | copy-start | bytes 2064388
  19.7 6.4 %collective-permute-start.1 = (bf16[1,10752]{1,0:T(2,128)(2,1)S(1)}, bf16[1,10752]{1,0:T(2,128)(2,1)S(1)}, u32[]{:S(2)}, u32[]{:S(2)}) collective-permute-start(bf16[1,10752]{1,0:T(2,128)(2,1)S(1)} %slice.440), channel_id=1, source_target_pairs={{0,4},{4,8},{8,12},{12,16},{16,20},{20,24},{24,28},{1,5},{5,9},{9,... | collective-permute-start | bytes 64520 | tf_op jit(solution)/shard_map/ppermute | solution.py:16
  24.5 4.7 %copy-start.29 = (f32[2,8]{1,0:T(2,128)}, f32[2,8]{1,0:T(2,128)S(1)}, u32[]{:S(2)}) copy-start(f32[2,8]{1,0:T(2,128)S(1)} %get-tuple-element.62) | copy-start | bytes 196
  24.5 72.2 %copy-start.27 = (f32[2,8]{1,0:T(2,128)}, f32[2,8]{1,0:T(2,128)S(1)}, u32[]{:S(2)}) copy-start(f32[2,8]{1,0:T(2,128)S(1)} %get-tuple-element.61) | copy-start | bytes 196
  26.2 1.2 copy-start.18
  27.1 0.8 copy-start.19
  27.1 0.8 copy-start.20
  27.9 0.7 copy-start.33
  31.1 15.1 %copy-start.31 = (f32[256]{0:T(256)S(1)}, f32[256]{0:T(256)}, u32[]{:S(2)}) copy-start(f32[256]{0:T(256)} %param.20) | copy-start | bytes 3076
  46.1 49.5 %copy-start.25 = (bf16[2,2,13,128,1]{3,2,1,0,4:T(8,128)(2,1)S(1)}, bf16[2,2,13,128,1]{3,2,1,0,4:T(8,128)(2,1)}, u32[]{:S(2)}) copy-start(bf16[2,2,13,128,1]{3,2,1,0,4:T(8,128)(2,1)} %constant.67) | copy-start | bytes 39940
  83.0 12.4 %all-to-all-start.1 = ((bf16[2,128,2,64]{1,2,0,3:T(2,128)(2,1)}), bf16[2,128,2,64]{1,2,0,3:T(2,128)(2,1)S(1)}, u32[]{:S(2)}, u32[]{:S(2)}) async-start(bf16[2,128,2,64]{1,2,0,3:T(2,128)(2,1)} %copy.61), calls=%async_computation.1 | async-start | bytes 131072 | tf_op jit(solution)/shard_map/all_to_all | solution.py:144
  88.5 74.7 %all-reduce.9.cloned.1.call-start = ((), (), s32[]{:S(2)}) async-start(), calls=%async_computation.5 | async-start | bytes 262144 | tf_op jit(solution)/shard_map/psum | solution.py:143
  96.7 1.0 copy-start.12
  96.7 1.1 copy-start.13
  97.8 1.0 copy-start.2
  97.8 2.5 %copy-start.5 = (f32[8,10752]{1,0:T(8,128)S(1)}, f32[8,10752]{1,0:T(8,128)}, u32[]{:S(2)}) copy-start(f32[8,10752]{1,0:T(8,128)} %param.17) | copy-start | bytes 1032196
  97.8 2.5 %copy-start.17 = (f32[8,10752]{1,0:T(8,128)S(1)}, f32[8,10752]{1,0:T(8,128)}, u32[]{:S(2)}) copy-start(f32[8,10752]{1,0:T(8,128)} %get-tuple-element.28) | copy-start | bytes 1032196
  98.9 5.9 %collective-permute-start.2 = (bf16[2,10752]{1,0:T(2,128)(2,1)S(1)}, bf16[2,10752]{1,0:T(2,128)(2,1)S(1)}, u32[]{:S(2)}, u32[]{:S(2)}) collective-permute-start(bf16[2,10752]{1,0:T(2,128)(2,1)S(1)} %pad_maximum_fusion.5), channel_id=1, source_target_pairs={{4,0},{8,4},{12,8},{16,12},{20,16},{24,20},{28,24},{5,1},{9,5},{13... | collective-permute-start | bytes 129032 | tf_op jit(solution)/shard_map/ppermute | solution.py:16
  101.1 3.8 %copy-start.7 = (f32[8,10752]{1,0:T(8,128)S(1)}, f32[8,10752]{1,0:T(8,128)}, u32[]{:S(2)}) copy-start(f32[8,10752]{1,0:T(8,128)} %get-tuple-element.42) | copy-start | bytes 1032196
  101.1 3.8 %copy-start.9 = (f32[8,10752]{1,0:T(8,128)S(1)}, f32[8,10752]{1,0:T(8,128)}, u32[]{:S(2)}) copy-start(f32[8,10752]{1,0:T(8,128)} %get-tuple-element.43) | copy-start | bytes 1032196
  101.1 3.8 %copy-start.24 = (f32[2,8,10752]{2,1,0:T(8,128)S(1)}, f32[2,8,10752]{2,1,0:T(8,128)}, u32[]{:S(2)}) copy-start(f32[2,8,10752]{2,1,0:T(8,128)} %param.13) | copy-start | bytes 2064388
  106.5 4.9 %collective-permute-start.3 = (bf16[2,10752]{1,0:T(2,128)(2,1)S(1)}, bf16[2,10752]{1,0:T(2,128)(2,1)S(1)}, u32[]{:S(2)}, u32[]{:S(2)}) collective-permute-start(bf16[2,10752]{1,0:T(2,128)(2,1)S(1)} %pad_maximum_fusion.6), channel_id=1, source_target_pairs={{0,4},{4,8},{8,12},{12,16},{16,20},{20,24},{24,28},{1,5},{5,9},{9,... | collective-permute-start | bytes 129032 | tf_op jit(solution)/shard_map/ppermute | solution.py:16
  111.9 0.8 copy-start.21
  112.7 0.7 copy-start.34
  112.7 1.2 copy-start.30
  115.8 13.2 %copy-start.32 = (f32[256]{0:T(256)S(1)}, f32[256]{0:T(256)}, u32[]{:S(2)}) copy-start(f32[256]{0:T(256)} %param.20) | copy-start | bytes 3076
  129.0 47.7 %copy-start.26 = (bf16[2,2,13,128,1]{3,2,1,0,4:T(8,128)(2,1)S(1)}, bf16[2,2,13,128,1]{3,2,1,0,4:T(8,128)(2,1)}, u32[]{:S(2)}) copy-start(bf16[2,2,13,128,1]{3,2,1,0,4:T(8,128)(2,1)} %constant.67) | copy-start | bytes 39940
  135.1 42.1 %copy-start.22 = (f32[84,128]{1,0:T(8,128)S(1)}, f32[84,128]{1,0:T(8,128)}, u32[]{:S(2)}) copy-start(f32[84,128]{1,0:T(8,128)} %constant.64) | copy-start | bytes 129028
  177.4 1.3 copy-start.28
  179.8 2.4 %copy-start.11 = (f32[1,8,10752]{2,1,0:T(8,128)S(1)}, f32[1,8,10752]{2,1,0:T(8,128)}, u32[]{:S(2)}) copy-start(f32[1,8,10752]{2,1,0:T(8,128)} %get-tuple-element.44) | copy-start | bytes 1032196
  179.9 2.4 %copy-start.14 = (f32[1,8,10752]{2,1,0:T(8,128)S(1)}, f32[1,8,10752]{2,1,0:T(8,128)}, u32[]{:S(2)}) copy-start(f32[1,8,10752]{2,1,0:T(8,128)} %get-tuple-element.4) | copy-start | bytes 1032196
  180.7 6.2 %copy-start.6 = (f32[8,10752]{1,0:T(8,128)S(1)}, f32[8,10752]{1,0:T(8,128)}, u32[]{:S(2)}) copy-start(f32[8,10752]{1,0:T(8,128)} %param.17) | copy-start | bytes 1032196
  180.7 6.2 %copy-start.8 = (f32[8,10752]{1,0:T(8,128)S(1)}, f32[8,10752]{1,0:T(8,128)}, u32[]{:S(2)}) copy-start(f32[8,10752]{1,0:T(8,128)} %get-tuple-element.42) | copy-start | bytes 1032196
  180.7 6.2 %copy-start.10 = (f32[8,10752]{1,0:T(8,128)S(1)}, f32[8,10752]{1,0:T(8,128)}, u32[]{:S(2)}) copy-start(f32[8,10752]{1,0:T(8,128)} %get-tuple-element.43) | copy-start | bytes 1032196
  180.7 6.2 %copy-start.15 = (f32[8,10752]{1,0:T(8,128)S(1)}, f32[8,10752]{1,0:T(8,128)}, u32[]{:S(2)}) copy-start(f32[8,10752]{1,0:T(8,128)} %get-tuple-element.21) | copy-start | bytes 1032196
  180.7 6.2 %copy-start.16 = (f32[8,10752]{1,0:T(8,128)S(1)}, f32[8,10752]{1,0:T(8,128)}, u32[]{:S(2)}) copy-start(f32[8,10752]{1,0:T(8,128)} %get-tuple-element.40) | copy-start | bytes 1032196
  180.8 6.0 %collective-permute-start.4 = (bf16[1,10752]{1,0:T(2,128)(2,1)S(1)}, bf16[1,10752]{1,0:T(2,128)(2,1)S(1)}, u32[]{:S(2)}, u32[]{:S(2)}) collective-permute-start(bf16[1,10752]{1,0:T(2,128)(2,1)S(1)} %slice.436), channel_id=1, source_target_pairs={{4,0},{8,4},{12,8},{16,12},{20,16},{24,20},{28,24},{5,1},{9,5},{13... | collective-permute-start | bytes 64520 | tf_op jit(solution)/shard_map/ppermute | solution.py:16
  187.3 4.9 %collective-permute-start.5 = (bf16[1,10752]{1,0:T(2,128)(2,1)S(1)}, bf16[1,10752]{1,0:T(2,128)(2,1)S(1)}, u32[]{:S(2)}, u32[]{:S(2)}) collective-permute-start(bf16[1,10752]{1,0:T(2,128)(2,1)S(1)} %slice.435), channel_id=1, source_target_pairs={{0,4},{4,8},{8,12},{12,16},{16,20},{20,24},{24,28},{1,5},{5,9},{9,... | collective-permute-start | bytes 64520 | tf_op jit(solution)/shard_map/ppermute | solution.py:16
Sparse Core Ops, SparseCore 0:
  52.3 28.9 all-reduce.6
  135.2 27.9 all-reduce.8
where the time goes:
time: 201 us; the launch traced here: 200 us
  waiting for transfers between devices  79.5 us (40%)
  blocking collectives  35.2 us (18%)
  starting transfers between devices  20.9 us (10%)
  local copies, waits for them, and re-layouts  20.4 us (10%)
  between operations  15 us (7%)
  matrix products  14.8 us (7%)
  other arithmetic  14.2 us (7%)
    psum x2, waiting for transfers between devices, on_device(): total_sum = lax.psum(partial_value.astype(jnp.bfloat16), 'deg')  57.2 us
    all_to_all x2, blocking collectives, on_device(): lax.all_to_all(spectra, 'lat', split_axis=1, concat_axis=3, tiled=True)  23 us
    ppermute x6, waiting for transfers between devices, passed_along(): return lax.ppermute(value, axis, pairs)  15.4 us
    ppermute x6, starting transfers between devices, passed_along(): return lax.ppermute(value, axis, pairs)  15.3 us
    all_to_all x1, blocking collectives, on_device(): lax.all_to_all(total_sum, 'lat', split_axis=3, concat_axis=1, tiled=True)  12.2 us
    dot_general x2, matrix products, legendre(): jnp.einsum('cmfl,mil->cmfi', scaled, basis, preferred_element_type=jnp.fl...  12 us
    unnamed x74, local copies, waits for them, and re-layouts  8.38 us
    all_to_all x1, waiting for transfers between devices, on_device(): lax.all_to_all(total_sum, 'lat', split_axis=3, concat_axis=1, tiled=True)  6.85 us
  transfers between devices with their start and end apart: 9, of which 9 were waited for; matrix products, arithmetic and copies ran while one was open for 2% of the time, Pallas kernels for 0%

commit v1 on v0

--- a/solution.py
+++ b/solution.py
@@ -141,7 +141,12 @@
         owned_rows = lax.all_to_all(spectra, "lat", split_axis=1, concat_axis=3, tiled=True)
         partial_value = legendre(owned_rows, basis, love)
         total_sum = lax.psum(partial_value.astype(jnp.bfloat16), "deg")
-        banded = lax.all_to_all(total_sum, "lat", split_axis=3, concat_axis=1, tiled=True)
+        banded = jnp.concatenate(
+            lax.all_to_all(
+                jnp.stack(jnp.split(total_sum, lax.axis_size("lat"), axis=3)), "lat", 0, 0
+            ),
+            axis=1,
+        )
         loads = synthesise(banded, full_factor, tables, output_weight)
         last = step_index == STEPS - 1
         psi_now = state_eta - loads[0]

time: 201 us -> 212 us (1.055)
  local copies, waits for them, and re-layouts: 20.4 us -> 29 us
    another operation x0 -> x20, local copies, waits for them, and re-layouts: none -> 7.17 us  [on_device(): jnp.stack(jnp.split(total_sum, lax.axis_size('lat'), axis=3))]
    unnamed x74 -> x88, local copies, waits for them, and re-layouts: 8.38 us -> 11.7 us
    psum x2 -> x0, local copies, waits for them, and re-layouts: 2.7 us -> none  [on_device(): total_sum = lax.psum(partial_value.astype(jnp.bfloat16), 'deg')]
where the time goes in v1:
time: 212 us; the launch traced here: 211 us
  waiting for transfers between devices  79.6 us (38%)
  blocking collectives  35.2 us (17%)
  local copies, waits for them, and re-layouts  29 us (14%)
  starting transfers between devices  20.9 us (10%)
  other arithmetic  16.1 us (8%)
  between operations  15 us (7%)
  matrix products  14.8 us (7%)
    psum x2, waiting for transfers between devices, on_device(): total_sum = lax.psum(partial_value.astype(jnp.bfloat16), 'deg')  57.3 us
    all_to_all x2, blocking collectives, on_device(): lax.all_to_all(spectra, 'lat', split_axis=1, concat_axis=3, tiled=True)  23 us
    ppermute x6, waiting for transfers between devices, passed_along(): return lax.ppermute(value, axis, pairs)  15.4 us
    ppermute x6, starting transfers between devices, passed_along(): return lax.ppermute(value, axis, pairs)  15.3 us
    all_to_all x1, blocking collectives, on_device(): lax.all_to_all(jnp.stack(jnp.split(total_sum, lax.axis_size('lat'), axis=...  12.2 us
    dot_general x2, matrix products, legendre(): jnp.einsum('cmfl,mil->cmfi', scaled, basis, preferred_element_type=jnp.fl...  12 us
    unnamed x88, local copies, waits for them, and re-layouts  11.7 us
    another operation x20, local copies, waits for them, and re-layouts, on_device(): jnp.stack(jnp.split(total_sum, lax.axis_size('lat'), axis=3))  7.17 us
  transfers between devices with their start and end apart: 9, of which 9 were waited for; matrix products, arithmetic and copies ran while one was open for 2% of the time, Pallas kernels for 0%

profile of v1, /device:TPU:0, one launch (start us, length us, event | category | flops | bytes accessed | tf_op | source)
XLA Modules:
  0.0 210.6 jit_solution(11826080757478202720)
XLA Ops:
  7.3 1.0 slice.442
  8.3 1.0 convert_element_type.99
  9.3 1.3 multiply_multiply_fusion.3
  10.8 1.3 collective-permute-start
  13.4 4.8 %collective-permute-done = bf16[3,10752]{1,0:T(4,128)(2,1)S(1)} collective-permute-done((bf16[3,10752]{1,0:T(4,128)(2,1)S(1)}, bf16[3,10752]{1,0:T(4,128)(2,1)S(1)}, u32[]{:S(2)}, u32[]{:S(2)}) %collective-permute-start) | collective-permute-done | bytes 64544 | tf_op jit(solution)/shard_map/ppermute | solution.py:16
  18.3 1.3 broadcast_multiply_fusion.3
  19.7 4.8 %collective-permute-start.1 = (bf16[1,10752]{1,0:T(2,128)(2,1)S(1)}, bf16[1,10752]{1,0:T(2,128)(2,1)S(1)}, u32[]{:S(2)}, u32[]{:S(2)}) collective-permute-start(bf16[1,10752]{1,0:T(2,128)(2,1)S(1)} %slice.440), channel_id=1, source_target_pairs={{0,4},{4,8},{8,12},{12,16},{16,20},{20,24},{24,28},{1,5},{5,9},{9,... | collective-permute-start | bytes 64520 | tf_op jit(solution)/shard_map/ppermute | solution.py:16
  24.6 1.6 collective-permute-done.1
  26.2 0.9 convert_bitcast_fusion.2
  29.3 0.7 copy.84
  30.0 1.1 reshape.120
  31.1 12.4 %all_to_all.46 = bf16[8,2,2048]{2,1,0:T(2,128)(2,1)S(1)} all-to-all(bf16[8,2,2048]{2,1,0:T(2,128)(2,1)S(1)} %reshape.120), channel_id=1, replica_groups=mesh['lat'=8,'deg'=4] {'lat'}, dimensions={0} | all-to-all | bytes 131072 | tf_op jit(solution)/shard_map/all_to_all | solution.py:141
  43.5 1.2 reshape.121
  44.7 1.3 copy.131
  46.2 6.0 %fusion.45 = bf16[2,128,2,64]{3,2,0,1:T(2,128)(2,1)} fusion(bf16[128,64,256]{2,1,0:T(8,128)(2,1)} %param.19, bf16[2,128,2,64]{3,2,0,1:T(2,128)(2,1)S(1)} %copy.87, f32[256]{0:T(256)S(1)} %copy-done.31), kind=kOutput, calls=%fused_computation.25 | convolution fusion | flops 33849344 | bytes 4326400 | tf_op jit(solution)/shard_map/cmfl,mil->cmfi/dot_general | solution.py:60
  52.2 29.1 %all-reduce.7.cloned.1.call-done = bf16[2,128,2,64]{3,2,0,1:T(2,128)(2,1)} async-done(((bf16[2,128,2,64]{3,2,0,1:T(2,128)(2,1)}), bf16[2,128,2,64]{3,2,0,1:T(2,128)(2,1)}) %all-reduce.7.cloned.1.call-update) | async-done | bytes 65552 | tf_op jit(solution)/shard_map/psum | solution.py:143
  81.3 2.6 %slice_bitcast_fusion.12 = (bf16[1,2,128,2,8]{4,3,1,2,0:T(2,128)(2,1)S(1)}, bf16[1,2,128,2,8]{4,3,1,2,0:T(2,128)(2,1)S(1)}, bf16[1,2,128,2,8]{4,3,1,2,0:T(2,128)...) fusion(bf16[2,128,2,64]{3,2,0,1:T(2,128)(2,1)} %all-reduce.7.cl, ...), kind=kLoop, calls=%fused_computation.148 | loop fusion | bytes 131072 | tf_op jit(solution)/shard_map/stack | solution.py:146
  89.4 5.5 %all-to-all-start.1 = ((bf16[8,2,128,2,8]{2,4,3,1,0:T(8,128)(2,1)}), bf16[8,2,128,2,8]{2,4,3,1,0:T(8,128)(2,1)S(1)}, u32[]{:S(2)}, u32[]{:S(2)}) async-start(bf16[8,2,128,2,8]{2,4,3,1,0:T(8,128)(2,1)} %constant_dynamic-update-slice_fusion), calls=%async_computation.1 | async-start | bytes 131072 | tf_op jit(solution)/shard_map/all_to_all | solution.py:145
  95.0 6.8 %all-to-all-done.1 = bf16[8,2,128,2,8]{2,4,3,1,0:T(8,128)(2,1)S(1)} async-done(((bf16[8,2,128,2,8]{2,4,3,1,0:T(8,128)(2,1)}), bf16[8,2,128,2,8]{2,4,3,1,0:T(8,128)(2,1)S(1)}, u32[]{:S(2)}, u32[]{:S(2)}) %all-to-all-start.1) | async-done | bytes 65568 | tf_op jit(solution)/shard_map/all_to_all | solution.py:145
  103.0 1.0 reshape.94
  104.0 1.3 broadcast_multiply_fusion.1
  105.6 0.7 copy-done.2
  106.4 1.3 collective-permute-start.2
  107.8 0.9 multiply_bitcast_fusion.1
  108.9 3.5 %collective-permute-done.2 = bf16[2,10752]{1,0:T(2,128)(2,1)S(1)} collective-permute-done((bf16[2,10752]{1,0:T(2,128)(2,1)S(1)}, bf16[2,10752]{1,0:T(2,128)(2,1)S(1)}, u32[]{:S(2)}, u32[]{:S(2)}) %collective-permute-start.2) | collective-permute-done | bytes 43040 | tf_op jit(solution)/shard_map/ppermute | solution.py:16
  112.4 1.3 fusion.128
  114.0 3.4 %collective-permute-start.3 = (bf16[2,10752]{1,0:T(2,128)(2,1)S(1)}, bf16[2,10752]{1,0:T(2,128)(2,1)S(1)}, u32[]{:S(2)}, u32[]{:S(2)}) collective-permute-start(bf16[2,10752]{1,0:T(2,128)(2,1)S(1)} %pad_maximum_fusion.6), channel_id=1, source_target_pairs={{0,4},{4,8},{8,12},{12,16},{16,20},{20,24},{24,28},{1,5},{5,9},{9,... | collective-permute-start | bytes 129032 | tf_op jit(solution)/shard_map/ppermute | solution.py:16
  117.5 1.3 collective-permute-done.3
  119.2 0.9 convert_bitcast_fusion
  122.2 0.7 copy.100
  123.0 1.1 reshape.122
  124.0 10.6 %all_to_all.47 = bf16[8,2,2048]{2,1,0:T(2,128)(2,1)S(1)} all-to-all(bf16[8,2,2048]{2,1,0:T(2,128)(2,1)S(1)} %reshape.122), channel_id=1, replica_groups=mesh['lat'=8,'deg'=4] {'lat'}, dimensions={0} | all-to-all | bytes 131072 | tf_op jit(solution)/shard_map/all_to_all | solution.py:141
  134.6 1.2 reshape.123
  135.8 1.3 copy.137
  137.3 6.0 %fusion.40 = bf16[2,128,2,64]{3,2,0,1:T(2,128)(2,1)} fusion(bf16[128,64,256]{2,1,0:T(8,128)(2,1)} %param.19, bf16[2,128,2,64]{3,2,0,1:T(2,128)(2,1)S(1)} %copy.103, f32[256]{0:T(256)S(1)} %copy-done.32), kind=kOutput, calls=%fused_computation.24 | convolution fusion | flops 33849344 | bytes 4326400 | tf_op jit(solution)/shard_map/cmfl,mil->cmfi/dot_general | solution.py:60
  143.3 28.2 %all-reduce.9.cloned.1.call-done = bf16[2,128,2,64]{3,2,0,1:T(2,128)(2,1)} async-done(((bf16[2,128,2,64]{3,2,0,1:T(2,128)(2,1)}), bf16[2,128,2,64]{3,2,0,1:T(2,128)(2,1)}) %all-reduce.9.cloned.1.call-update) | async-done | bytes 65552 | tf_op jit(solution)/shard_map/psum | solution.py:143
  171.5 2.6 %slice_bitcast_fusion.4 = (bf16[1,2,128,2,8]{4,3,1,2,0:T(2,128)(2,1)S(1)}, bf16[1,2,128,2,8]{4,3,1,2,0:T(2,128)(2,1)S(1)}, bf16[1,2,128,2,8]{4,3,1,2,0:T(2,128)(...) fusion(bf16[2,128,2,64]{3,2,0,1:T(2,128)(2,1)} %all-reduce.9.cl, ...), kind=kLoop, calls=%fused_computation.138 | loop fusion | bytes 131072 | tf_op jit(solution)/shard_map/stack | solution.py:146
  174.9 12.2 %all_to_all.48 = bf16[8,2,128,2,8]{2,4,3,1,0:T(8,128)(2,1)S(1)} all-to-all(bf16[8,2,128,2,8]{2,4,3,1,0:T(8,128)(2,1)S(1)} %constant_dynamic-update-slice_fusion.8), channel_id=1, replica_groups=mesh['lat'=8,'deg'=4] {'lat'}, dimensions={0} | all-to-all | bytes 131072 | tf_op jit(solution)/shard_map/all_to_all | solution.py:145
  188.3 1.0 reshape.99
  189.2 1.3 broadcast_multiply_fusion
  190.5 0.8 fusion.62
  191.4 1.4 collective-permute-start.4
  192.8 0.9 pad_maximum_fusion.1
  193.9 3.5 %collective-permute-done.4 = bf16[1,10752]{1,0:T(2,128)(2,1)S(1)} collective-permute-done((bf16[1,10752]{1,0:T(2,128)(2,1)S(1)}, bf16[1,10752]{1,0:T(2,128)(2,1)S(1)}, u32[]{:S(2)}, u32[]{:S(2)}) %collective-permute-start.4) | collective-permute-done | bytes 21536 | tf_op jit(solution)/shard_map/ppermute | solution.py:16
  197.9 3.2 %collective-permute-start.5 = (bf16[1,10752]{1,0:T(2,128)(2,1)S(1)}, bf16[1,10752]{1,0:T(2,128)(2,1)S(1)}, u32[]{:S(2)}, u32[]{:S(2)}) collective-permute-start(bf16[1,10752]{1,0:T(2,128)(2,1)S(1)} %slice.435), channel_id=1, source_target_pairs={{0,4},{4,8},{8,12},{12,16},{16,20},{20,24},{24,28},{1,5},{5,9},{9,... | collective-permute-start | bytes 64520 | tf_op jit(solution)/shard_map/ppermute | solution.py:16
  201.1 0.9 pad_maximum_fusion
  202.1 0.7 collective-permute-done.5
  202.8 0.9 fusion.101
  (183 shorter events, 16.9 us)
Async XLA Ops:
  7.2 74.1 %all-reduce.7.cloned.1.call-start = ((), (), s32[]{:S(2)}) async-start(), calls=%async_computation.4 | async-start | bytes 262144 | tf_op jit(solution)/shard_map/psum | solution.py:143
  9.3 3.1 %copy-start.1 = (f32[8,10752]{1,0:T(8,128)}, f32[8,10752]{1,0:T(8,128)S(1)}, u32[]{:S(2)}) copy-start(f32[8,10752]{1,0:T(8,128)S(1)} %convert_element_type.99) | copy-start | bytes 1032196
  9.3 3.0 %copy-start.3 = (f32[8,10752]{1,0:T(8,128)S(1)}, f32[8,10752]{1,0:T(8,128)}, u32[]{:S(2)}) copy-start(f32[8,10752]{1,0:T(8,128)} %param.16) | copy-start | bytes 1032196
  10.8 7.4 %collective-permute-start = (bf16[3,10752]{1,0:T(4,128)(2,1)S(1)}, bf16[3,10752]{1,0:T(4,128)(2,1)S(1)}, u32[]{:S(2)}, u32[]{:S(2)}) collective-permute-start(bf16[3,10752]{1,0:T(4,128)(2,1)S(1)} %pad_maximum_fusion.4), channel_id=1, source_target_pairs={{4,0},{8,4},{12,8},{16,12},{20,16},{24,20},{28,24},{5,1},{9,5},{13... | collective-permute-start | bytes 193544 | tf_op jit(solution)/shard_map/ppermute | solution.py:16
  12.4 1.0 copy-start.4
  12.5 5.8 %copy-start = (s32[8,10752]{1,0:T(8,128)S(1)}, s32[8,10752]{1,0:T(8,128)}, u32[]{:S(2)}) copy-start(s32[8,10752]{1,0:T(8,128)} %param.18) | copy-start | bytes 1032196
  12.5 5.8 %slice-start = ((f32[8,10752]{1,0:T(8,128)}), f32[8,1]{1,0:T(8,128)S(1)}, s32[]{:S(2)}) async-start(f32[8,10752]{1,0:T(8,128)} %copy-done.1), calls=%async_computation.6 | async-start | bytes 8192 | tf_op jit(solution)/shard_map/jit(_roll_static)/slice | solution.py:110
  12.5 5.8 %slice-start.1 = ((f32[8,10752]{1,0:T(8,128)}), f32[8,1]{1,0:T(8,128)S(1)}, s32[]{:S(2)}) async-start(f32[8,10752]{1,0:T(8,128)} %param.16), calls=%async_computation.7 | async-start | bytes 8192 | tf_op jit(solution)/shard_map/jit(_roll_static)/slice | solution.py:112
  12.6 5.8 %copy-start.23 = (f32[2,8,10752]{2,1,0:T(8,128)S(1)}, f32[2,8,10752]{2,1,0:T(8,128)}, u32[]{:S(2)}) copy-start(f32[2,8,10752]{2,1,0:T(8,128)} %param.15) | copy-start | bytes 2064388
  19.7 6.4 %collective-permute-start.1 = (bf16[1,10752]{1,0:T(2,128)(2,1)S(1)}, bf16[1,10752]{1,0:T(2,128)(2,1)S(1)}, u32[]{:S(2)}, u32[]{:S(2)}) collective-permute-start(bf16[1,10752]{1,0:T(2,128)(2,1)S(1)} %slice.440), channel_id=1, source_target_pairs={{0,4},{4,8},{8,12},{12,16},{16,20},{20,24},{24,28},{1,5},{5,9},{9,... | collective-permute-start | bytes 64520 | tf_op jit(solution)/shard_map/ppermute | solution.py:16
  24.5 4.7 %copy-start.29 = (f32[2,8]{1,0:T(2,128)}, f32[2,8]{1,0:T(2,128)S(1)}, u32[]{:S(2)}) copy-start(f32[2,8]{1,0:T(2,128)S(1)} %get-tuple-element.78) | copy-start | bytes 196
  24.5 79.5 %copy-start.27 = (f32[2,8]{1,0:T(2,128)}, f32[2,8]{1,0:T(2,128)S(1)}, u32[]{:S(2)}) copy-start(f32[2,8]{1,0:T(2,128)S(1)} %get-tuple-element.77) | copy-start | bytes 196
  26.2 1.2 copy-start.18
  27.1 0.8 copy-start.19
  27.1 0.8 copy-start.20
  28.0 0.7 copy-start.33
  31.1 15.1 %copy-start.31 = (f32[256]{0:T(256)S(1)}, f32[256]{0:T(256)}, u32[]{:S(2)}) copy-start(f32[256]{0:T(256)} %param.20) | copy-start | bytes 3076
  83.9 18.2 %copy-start.25 = (bf16[2,2,13,128,1]{3,2,1,0,4:T(8,128)(2,1)S(1)}, bf16[2,2,13,128,1]{3,2,1,0,4:T(8,128)(2,1)}, u32[]{:S(2)}) copy-start(bf16[2,2,13,128,1]{3,2,1,0,4:T(8,128)(2,1)} %constant.67) | copy-start | bytes 39940
  89.4 12.4 %all-to-all-start.1 = ((bf16[8,2,128,2,8]{2,4,3,1,0:T(8,128)(2,1)}), bf16[8,2,128,2,8]{2,4,3,1,0:T(8,128)(2,1)S(1)}, u32[]{:S(2)}, u32[]{:S(2)}) async-start(bf16[8,2,128,2,8]{2,4,3,1,0:T(8,128)(2,1)} %constant_dynamic-update-slice_fusion), calls=%async_computation.1 | async-start | bytes 131072 | tf_op jit(solution)/shard_map/all_to_all | solution.py:145
  94.9 76.5 %all-reduce.9.cloned.1.call-start = ((), (), s32[]{:S(2)}) async-start(), calls=%async_computation.5 | async-start | bytes 262144 | tf_op jit(solution)/shard_map/psum | solution.py:143
  103.9 1.3 copy-start.11
  104.0 1.3 copy-start.12
  105.3 1.0 copy-start.2
  105.3 2.5 %copy-start.5 = (f32[8,10752]{1,0:T(8,128)S(1)}, f32[8,10752]{1,0:T(8,128)}, u32[]{:S(2)}) copy-start(f32[8,10752]{1,0:T(8,128)} %param.17) | copy-start | bytes 1032196
  105.3 2.5 %copy-start.17 = (f32[8,10752]{1,0:T(8,128)S(1)}, f32[8,10752]{1,0:T(8,128)}, u32[]{:S(2)}) copy-start(f32[8,10752]{1,0:T(8,128)} %get-tuple-element.28) | copy-start | bytes 1032196
  106.4 5.9 %collective-permute-start.2 = (bf16[2,10752]{1,0:T(2,128)(2,1)S(1)}, bf16[2,10752]{1,0:T(2,128)(2,1)S(1)}, u32[]{:S(2)}, u32[]{:S(2)}) collective-permute-start(bf16[2,10752]{1,0:T(2,128)(2,1)S(1)} %pad_maximum_fusion.5), channel_id=1, source_target_pairs={{4,0},{8,4},{12,8},{16,12},{20,16},{24,20},{28,24},{5,1},{9,5},{13... | collective-permute-start | bytes 129032 | tf_op jit(solution)/shard_map/ppermute | solution.py:16
  108.6 3.8 %copy-start.6 = (f32[8,10752]{1,0:T(8,128)S(1)}, f32[8,10752]{1,0:T(8,128)}, u32[]{:S(2)}) copy-start(f32[8,10752]{1,0:T(8,128)} %get-tuple-element.42) | copy-start | bytes 1032196
  108.6 3.8 %copy-start.8 = (f32[8,10752]{1,0:T(8,128)S(1)}, f32[8,10752]{1,0:T(8,128)}, u32[]{:S(2)}) copy-start(f32[8,10752]{1,0:T(8,128)} %get-tuple-element.43) | copy-start | bytes 1032196
  108.6 3.8 %copy-start.24 = (f32[2,8,10752]{2,1,0:T(8,128)S(1)}, f32[2,8,10752]{2,1,0:T(8,128)}, u32[]{:S(2)}) copy-start(f32[2,8,10752]{2,1,0:T(8,128)} %param.13) | copy-start | bytes 2064388
  114.0 4.9 %collective-permute-start.3 = (bf16[2,10752]{1,0:T(2,128)(2,1)S(1)}, bf16[2,10752]{1,0:T(2,128)(2,1)S(1)}, u32[]{:S(2)}, u32[]{:S(2)}) collective-permute-start(bf16[2,10752]{1,0:T(2,128)(2,1)S(1)} %pad_maximum_fusion.6), channel_id=1, source_target_pairs={{0,4},{4,8},{8,12},{12,16},{16,20},{20,24},{24,28},{1,5},{5,9},{9,... | collective-permute-start | bytes 129032 | tf_op jit(solution)/shard_map/ppermute | solution.py:16
  120.1 0.8 copy-start.21
  120.9 0.7 copy-start.34
  120.9 1.2 copy-start.30
  124.0 13.2 %copy-start.32 = (f32[256]{0:T(256)S(1)}, f32[256]{0:T(256)}, u32[]{:S(2)}) copy-start(f32[256]{0:T(256)} %param.20) | copy-start | bytes 3076
  174.1 13.2 %copy-start.26 = (bf16[2,2,13,128,1]{3,2,1,0,4:T(8,128)(2,1)S(1)}, bf16[2,2,13,128,1]{3,2,1,0,4:T(8,128)(2,1)}, u32[]{:S(2)}) copy-start(bf16[2,2,13,128,1]{3,2,1,0,4:T(8,128)(2,1)} %constant.67) | copy-start | bytes 39940
  174.4 13.3 %copy-start.22 = (f32[84,128]{1,0:T(8,128)S(1)}, f32[84,128]{1,0:T(8,128)}, u32[]{:S(2)}) copy-start(f32[84,128]{1,0:T(8,128)} %constant.64) | copy-start | bytes 129028
  187.9 1.3 copy-start.28
  189.2 1.3 copy-start.13
  190.5 2.3 %copy-start.10 = (f32[1,8,10752]{2,1,0:T(8,128)S(1)}, f32[1,8,10752]{2,1,0:T(8,128)}, u32[]{:S(2)}) copy-start(f32[1,8,10752]{2,1,0:T(8,128)} %get-tuple-element.44) | copy-start | bytes 1032196
  190.5 2.3 %copy-start.14 = (f32[1,8,10752]{2,1,0:T(8,128)S(1)}, f32[1,8,10752]{2,1,0:T(8,128)}, u32[]{:S(2)}) copy-start(f32[1,8,10752]{2,1,0:T(8,128)} %get-tuple-element.4) | copy-start | bytes 1032196
  191.4 6.1 %copy-start.7 = (f32[8,10752]{1,0:T(8,128)S(1)}, f32[8,10752]{1,0:T(8,128)}, u32[]{:S(2)}) copy-start(f32[8,10752]{1,0:T(8,128)} %get-tuple-element.42) | copy-start | bytes 1032196
  191.4 6.1 %copy-start.9 = (f32[8,10752]{1,0:T(8,128)S(1)}, f32[8,10752]{1,0:T(8,128)}, u32[]{:S(2)}) copy-start(f32[8,10752]{1,0:T(8,128)} %get-tuple-element.43) | copy-start | bytes 1032196
  191.4 6.1 %copy-start.15 = (f32[8,10752]{1,0:T(8,128)S(1)}, f32[8,10752]{1,0:T(8,128)}, u32[]{:S(2)}) copy-start(f32[8,10752]{1,0:T(8,128)} %get-tuple-element.21) | copy-start | bytes 1032196
  191.4 6.1 %copy-start.16 = (f32[8,10752]{1,0:T(8,128)S(1)}, f32[8,10752]{1,0:T(8,128)}, u32[]{:S(2)}) copy-start(f32[8,10752]{1,0:T(8,128)} %get-tuple-element.40) | copy-start | bytes 1032196
  191.4 6.0 %collective-permute-start.4 = (bf16[1,10752]{1,0:T(2,128)(2,1)S(1)}, bf16[1,10752]{1,0:T(2,128)(2,1)S(1)}, u32[]{:S(2)}, u32[]{:S(2)}) collective-permute-start(bf16[1,10752]{1,0:T(2,128)(2,1)S(1)} %slice.436), channel_id=1, source_target_pairs={{4,0},{8,4},{12,8},{16,12},{20,16},{24,20},{28,24},{5,1},{9,5},{13... | collective-permute-start | bytes 64520 | tf_op jit(solution)/shard_map/ppermute | solution.py:16
  197.9 4.9 %collective-permute-start.5 = (bf16[1,10752]{1,0:T(2,128)(2,1)S(1)}, bf16[1,10752]{1,0:T(2,128)(2,1)S(1)}, u32[]{:S(2)}, u32[]{:S(2)}) collective-permute-start(bf16[1,10752]{1,0:T(2,128)(2,1)S(1)} %slice.435), channel_id=1, source_target_pairs={{0,4},{4,8},{8,12},{12,16},{16,20},{20,24},{24,28},{1,5},{5,9},{9,... | collective-permute-start | bytes 64520 | tf_op jit(solution)/shard_map/ppermute | solution.py:16
Sparse Core Ops, SparseCore 0:
  52.3 28.9 all-reduce.6
  143.4 27.9 all-reduce.8
